TPU v7x, 32 devices: a whole 2x2x4 slice. The times are simulated.
32 devices in a mesh: row: 2 (over core), nbr: 4 (over y, x), feat: 4 (over z).
Axes of the slice: x: 2, y: 2, z: 4, core: 2. Of those that a mesh axis runs over, the one named last changes fastest.
Arguments:
- features: float32 [1024, 8192], P('feat', 'nbr'), may hold values from -6 to 6
- tile_list: int32 [2, 4, 2, 256], P('row', 'nbr'), may hold values from 0 to 15, as said below
- tile_count: int32 [2, 4], P('row', 'nbr'), may hold values from 96 to 256
- weight: float32 [1024, 1024], P(('row', 'nbr'), 'feat'), may hold values from -0.1875 to 0.1875
- cotangent: float32 [4096, 1024], P(('row', 'nbr'), 'feat'), may hold values from -6 to 6
Outputs:
- activations: float32 [4096, 1024], P(('row', 'nbr'), 'feat')
- feature_grad: float32 [1024, 8192], P('feat', 'nbr')
- weight_grad: float32 [1024, 1024], P(('row', 'nbr'), 'feat')
Inputs may be any that keep to these rules, and one draw needn't show every extreme that they name: `tile_list`: each device's list names every (row block, column block) pair of its block exactly once; only the first tile_count entries are used.
All inputs are finite; a program needn't handle non-finite values.
Results may differ from a plain program's by a relative error of at most 0.0003.
Values sent between devices are 32-bit elements; how exact they have to be, the bound alone decides.
A program may use at most 64 MiB of HBM per device.

v0:
```python
import jax
import jax.numpy as jnp
from jax import lax
from jax.sharding import PartitionSpec as P

TILE = 128


modulus = 32749
highest = lax.Precision.HIGHEST
tile_batch = 32


def edge_value(row_index, col_index):
    hashed = (
        row_index * row_index % modulus * 3
        + col_index * col_index % modulus * 5
        + row_index * col_index % modulus * 7
        + row_index * 11
        + col_index * 13
    ) % modulus
    return hashed.astype(jnp.float32) / modulus - 0.5


def edge_tiles(row_picks, col_picks, row_base, col_base, tile, edge_scale):
    offsets = jnp.arange(tile, dtype=jnp.int32)
    rows_global = row_base + row_picks[:, None, None] * tile + offsets[None, :, None]
    cols_global = col_base + col_picks[:, None, None] * tile + offsets[None, None, :]
    return edge_value(rows_global, cols_global) * edge_scale


def tile_product(
    pairs, first_slot, end_slot, row_base, col_base, source, target_blocks, transpose, edge_scale
):
    tile = source.shape[1]
    width = source.shape[2]
    slots = pairs.shape[1]
    turns = jnp.maximum(end_slot - first_slot + tile_batch - 1, 0) // tile_batch

    def advance(block_turn, running):
        positions = first_slot + block_turn * tile_batch + jnp.arange(tile_batch, dtype=jnp.int32)
        in_range = positions < end_slot
        positions = jnp.minimum(positions, slots - 1)
        row_picks = pairs[0][positions]
        col_picks = pairs[1][positions]
        values = edge_tiles(row_picks, col_picks, row_base, col_base, tile, edge_scale)
        values = jnp.where(in_range[:, None, None], values, 0.0)
        if transpose:
            product = jnp.einsum("tab,taf->tbf", values, source[row_picks], precision=highest)
            target_picks = col_picks
        else:
            product = jnp.einsum("tab,tbf->taf", values, source[col_picks], precision=highest)
            target_picks = row_picks
        placing = (
            target_picks[None, :] == jnp.arange(target_blocks, dtype=jnp.int32)[:, None]
        ).astype(jnp.float32)
        return running + jnp.dot(
            placing, product.reshape(tile_batch, tile * width), precision=highest
        )

    running = lax.fori_loop(
        0, turns, advance, jnp.zeros((target_blocks, tile * width), jnp.float32)
    )
    return running.reshape(target_blocks * tile, width)


def per_device(features, tile_list, tile_count, weight, cotangent):
    pairs = tile_list[0, 0]
    tile_total = tile_count[0, 0]
    n_nbr = lax.axis_size("nbr")
    row_id = lax.axis_index("row")
    nbr_id = lax.axis_index("nbr")
    width = features.shape[0]
    c_dev = features.shape[1]
    r_dev = cotangent.shape[0] * n_nbr
    edge_scale = (12.0 / (c_dev * n_nbr / 2)) ** 0.5
    col_base = nbr_id * c_dev
    source = features.T.reshape(c_dev // TILE, TILE, width)
    row_blocks = r_dev // TILE
    partial_value = tile_product(
        pairs, 0, tile_total, row_id * r_dev, col_base, source, row_blocks, False, edge_scale
    )
    hidden = lax.psum_scatter(partial_value, "nbr", scatter_dimension=0, tiled=True)
    weight_cols = lax.all_gather(weight, ("row", "nbr"), axis=0, tiled=True)
    hidden_all = lax.all_gather(hidden, "feat", axis=1, tiled=True)
    pre_act = jnp.dot(hidden_all, weight_cols, precision=highest)
    squash = jax.nn.sigmoid(pre_act)
    activations = pre_act * squash
    grad_pre = cotangent * squash * (1.0 + pre_act * (1.0 - squash))
    grad_hidden = lax.psum_scatter(
        jnp.dot(grad_pre, weight_cols.T, precision=highest), "feat", scatter_dimension=1, tiled=True
    )
    weight_terms = jnp.dot(hidden_all.T, grad_pre, precision=highest)
    weight_grad = lax.psum_scatter(weight_terms, ("row", "nbr"), scatter_dimension=0, tiled=True)
    grad_block = lax.all_gather(grad_hidden, "nbr", axis=0, tiled=True)
    column_part = tile_product(
        pairs,
        0,
        tile_total,
        row_id * r_dev,
        col_base,
        grad_block.reshape(row_blocks, TILE, width),
        c_dev // TILE,
        True,
        edge_scale,
    )
    feature_grad = lax.psum(column_part.T, "row")
    return (activations, feature_grad, weight_grad)


def solution(mesh):
    in_specs = (
        P("feat", "nbr"),
        P("row", "nbr", None, None),
        P("row", "nbr"),
        P(("row", "nbr"), "feat"),
        P(("row", "nbr"), "feat"),
    )
    out_specs = (P(("row", "nbr"), "feat"), P("feat", "nbr"), P(("row", "nbr"), "feat"))
    return jax.shard_map(
        per_device, mesh=mesh, in_specs=in_specs, out_specs=out_specs, check_vma=False
    )
```

profile of v0, /device:TPU:0, one launch (start us, length us, event | category | flops | bytes accessed | tf_op | source)
XLA Modules:
  0.0 578.3 jit_solution(7663981763945907471)
XLA Ops:
  12.1 171.0 %while.24 = (s32[]{:T(128)}, f32[16,32768]{1,0:T(8,128)}, s32[]{:T(128)}, s32[2,256]{1,0:T(2,128)S(1)}, s32[]{:T(128)}, /*index=5*/s32[]{:T(128)}, s32[]{:T(128)}, f32[16,128,256]{2,1,0:T(8,128)S(1)}, s32[]{:T(128)}, s32[]{:T(128)}) while((s32[]{:T(128)}, f32[16,32768]{1,0:T(8,128)}, s32[]{:T(128)}, s32[2,256]{1,0:T(2,128)S(1)}, s32[]{:T(128)}, ...), condition=%wide.region_1.2_spmd, body=%wide.region_0.1_spmd.sunk | while | flops 1824607232 | bytes 50543228 | solution.py:61
  14.5 2.8 gather_fusion.1
  17.2 9.8 %fusion.133 = f32[32,128,256]{2,1,0:T(8,128)S(1)} fusion(f32[32,128,256]{2,1,0:T(8,128)} %gather_fusion.1, s32[32,128]{1,0:T(8,128)S(1)} %get-tuple-element.389, s32[32,128]{1,0:T(8,128)S(1)} %get-tuple-element.391, s32[32,128]{1,0:T(8,128)S(1)} %get-tuple-element.392, s32[32,128]{1,0:T(8,128)S(1)} %get-tuple-element.393, ...), kind=kOutput, calls=%fused_computation.19.clone.1 | convolution fusion | flops 1622671360 | bytes 8486944 | tf_op jit(solution)/shard_map/while/body/tab,tbf->taf/dot_general | solution.py:52
  29.5 2.7 convolution_add_fusion.4
  35.8 2.8 gather_fusion.1
  38.6 9.8 %fusion.133 = f32[32,128,256]{2,1,0:T(8,128)S(1)} fusion(f32[32,128,256]{2,1,0:T(8,128)} %gather_fusion.1, s32[32,128]{1,0:T(8,128)S(1)} %get-tuple-element.389, s32[32,128]{1,0:T(8,128)S(1)} %get-tuple-element.391, s32[32,128]{1,0:T(8,128)S(1)} %get-tuple-element.392, s32[32,128]{1,0:T(8,128)S(1)} %get-tuple-element.393, ...), kind=kOutput, calls=%fused_computation.19.clone.1 | convolution fusion | flops 1622671360 | bytes 8486944 | tf_op jit(solution)/shard_map/while/body/tab,tbf->taf/dot_general | solution.py:52
  50.8 2.7 convolution_add_fusion.4
  57.2 2.8 gather_fusion.1
  60.0 9.8 %fusion.133 = f32[32,128,256]{2,1,0:T(8,128)S(1)} fusion(f32[32,128,256]{2,1,0:T(8,128)} %gather_fusion.1, s32[32,128]{1,0:T(8,128)S(1)} %get-tuple-element.389, s32[32,128]{1,0:T(8,128)S(1)} %get-tuple-element.391, s32[32,128]{1,0:T(8,128)S(1)} %get-tuple-element.392, s32[32,128]{1,0:T(8,128)S(1)} %get-tuple-element.393, ...), kind=kOutput, calls=%fused_computation.19.clone.1 | convolution fusion | flops 1622671360 | bytes 8486944 | tf_op jit(solution)/shard_map/while/body/tab,tbf->taf/dot_general | solution.py:52
  72.2 2.7 convolution_add_fusion.4
  78.6 2.8 gather_fusion.1
  81.3 9.8 %fusion.133 = f32[32,128,256]{2,1,0:T(8,128)S(1)} fusion(f32[32,128,256]{2,1,0:T(8,128)} %gather_fusion.1, s32[32,128]{1,0:T(8,128)S(1)} %get-tuple-element.389, s32[32,128]{1,0:T(8,128)S(1)} %get-tuple-element.391, s32[32,128]{1,0:T(8,128)S(1)} %get-tuple-element.392, s32[32,128]{1,0:T(8,128)S(1)} %get-tuple-element.393, ...), kind=kOutput, calls=%fused_computation.19.clone.1 | convolution fusion | flops 1622671360 | bytes 8486944 | tf_op jit(solution)/shard_map/while/body/tab,tbf->taf/dot_general | solution.py:52
  99.9 2.8 gather_fusion.1
  102.7 9.8 %fusion.133 = f32[32,128,256]{2,1,0:T(8,128)S(1)} fusion(f32[32,128,256]{2,1,0:T(8,128)} %gather_fusion.1, s32[32,128]{1,0:T(8,128)S(1)} %get-tuple-element.389, s32[32,128]{1,0:T(8,128)S(1)} %get-tuple-element.391, s32[32,128]{1,0:T(8,128)S(1)} %get-tuple-element.392, s32[32,128]{1,0:T(8,128)S(1)} %get-tuple-element.393, ...), kind=kOutput, calls=%fused_computation.19.clone.1 | convolution fusion | flops 1622671360 | bytes 8486944 | tf_op jit(solution)/shard_map/while/body/tab,tbf->taf/dot_general | solution.py:52
  121.3 2.8 gather_fusion.1
  124.1 9.8 %fusion.133 = f32[32,128,256]{2,1,0:T(8,128)S(1)} fusion(f32[32,128,256]{2,1,0:T(8,128)} %gather_fusion.1, s32[32,128]{1,0:T(8,128)S(1)} %get-tuple-element.389, s32[32,128]{1,0:T(8,128)S(1)} %get-tuple-element.391, s32[32,128]{1,0:T(8,128)S(1)} %get-tuple-element.392, s32[32,128]{1,0:T(8,128)S(1)} %get-tuple-element.393, ...), kind=kOutput, calls=%fused_computation.19.clone.1 | convolution fusion | flops 1622671360 | bytes 8486944 | tf_op jit(solution)/shard_map/while/body/tab,tbf->taf/dot_general | solution.py:52
  142.7 2.8 gather_fusion.1
  145.5 9.8 %fusion.133 = f32[32,128,256]{2,1,0:T(8,128)S(1)} fusion(f32[32,128,256]{2,1,0:T(8,128)} %gather_fusion.1, s32[32,128]{1,0:T(8,128)S(1)} %get-tuple-element.389, s32[32,128]{1,0:T(8,128)S(1)} %get-tuple-element.391, s32[32,128]{1,0:T(8,128)S(1)} %get-tuple-element.392, s32[32,128]{1,0:T(8,128)S(1)} %get-tuple-element.393, ...), kind=kOutput, calls=%fused_computation.19.clone.1 | convolution fusion | flops 1622671360 | bytes 8486944 | tf_op jit(solution)/shard_map/while/body/tab,tbf->taf/dot_general | solution.py:52
  164.1 2.8 gather_fusion.1
  166.8 9.8 %fusion.133 = f32[32,128,256]{2,1,0:T(8,128)S(1)} fusion(f32[32,128,256]{2,1,0:T(8,128)} %gather_fusion.1, s32[32,128]{1,0:T(8,128)S(1)} %get-tuple-element.389, s32[32,128]{1,0:T(8,128)S(1)} %get-tuple-element.391, s32[32,128]{1,0:T(8,128)S(1)} %get-tuple-element.392, s32[32,128]{1,0:T(8,128)S(1)} %get-tuple-element.393, ...), kind=kOutput, calls=%fused_computation.19.clone.1 | convolution fusion | flops 1622671360 | bytes 8486944 | tf_op jit(solution)/shard_map/while/body/tab,tbf->taf/dot_general | solution.py:52
  183.1 2.7 reshape.453
  186.5 36.9 %reduce-scatter.4.cloned.1.call-done = f32[512,256]{1,0:T(8,128)} async-done(((f32[2048,256]{1,0:T(8,128)}), f32[512,256]{1,0:T(8,128)}) %reduce-scatter.4.cloned.1.call-update) | async-done | bytes 524304 | tf_op jit(solution)/shard_map/reduce_scatter | solution.py:83
  223.5 45.6 %all-gather.4.cloned.1.call-done = f32[512,1024]{1,0:T(8,128)} async-done(((f32[512,256]{1,0:T(8,128)}), f32[512,1024]{1,0:T(8,128)}) %all-gather.4.cloned.1.call-update) | async-done | bytes 2097168 | tf_op jit(solution)/shard_map/all_gather | solution.py:85
  269.1 4.5 fusion.94
  273.6 3.3 fusion.96
  277.0 42.4 %reduce-scatter.6.cloned.1.call-done = f32[512,256]{1,0:T(8,128)} async-done(((f32[512,1024]{1,0:T(8,128)}), f32[512,256]{1,0:T(8,128)}) %reduce-scatter.6.cloned.1.call-update) | async-done | bytes 524304 | tf_op jit(solution)/shard_map/reduce_scatter | solution.py:90
  319.6 34.4 %all-gather.8.cloned.1.call-done = f32[2048,256]{1,0:T(8,128)} async-done(((f32[512,256]{1,0:T(8,128)}), f32[2048,256]{1,0:T(8,128)}) %all-gather.8.cloned.1.call-update) | async-done | bytes 2097168 | tf_op jit(solution)/shard_map/all_gather | solution.py:95
  356.4 170.5 %while.25 = (s32[]{:T(128)}, f32[16,32768]{1,0:T(8,128)}, s32[]{:T(128)}, s32[2,256]{1,0:T(2,128)S(1)}, s32[]{:T(128)}, /*index=5*/s32[]{:T(128)}, s32[]{:T(128)}, f32[16,128,256]{2,1,0:T(8,128)S(1)}, s32[]{:T(128)}, s32[]{:T(128)}) while((s32[]{:T(128)}, f32[16,32768]{1,0:T(8,128)}, s32[]{:T(128)}, s32[2,256]{1,0:T(2,128)S(1)}, s32[]{:T(128)}, ...), condition=%wide.region_5.6_spmd, body=%wide.region_4.5_spmd.sunk | while | flops 1824607232 | bytes 50543228 | solution.py:61
  358.8 2.8 gather_fusion.4
  361.5 9.7 %fusion.142 = f32[32,128,256]{2,1,0:T(8,128)S(1)} fusion(f32[32,128,256]{2,1,0:T(8,128)} %gather_fusion.4, s32[32,128]{1,0:T(8,128)S(1)} %get-tuple-element.407, s32[32,128]{1,0:T(8,128)S(1)} %get-tuple-element.409, s32[32,128]{1,0:T(8,128)S(1)} %get-tuple-element.410, s32[32,128]{1,0:T(8,128)S(1)} %get-tuple-element.411, ...), kind=kOutput, calls=%fused_computation.82.clone.1 | convolution fusion | flops 1622671360 | bytes 8486944 | tf_op jit(solution)/shard_map/while/body/tab,taf->tbf/dot_general | solution.py:49
  380.1 2.8 gather_fusion.4
  382.9 9.7 %fusion.142 = f32[32,128,256]{2,1,0:T(8,128)S(1)} fusion(f32[32,128,256]{2,1,0:T(8,128)} %gather_fusion.4, s32[32,128]{1,0:T(8,128)S(1)} %get-tuple-element.407, s32[32,128]{1,0:T(8,128)S(1)} %get-tuple-element.409, s32[32,128]{1,0:T(8,128)S(1)} %get-tuple-element.410, s32[32,128]{1,0:T(8,128)S(1)} %get-tuple-element.411, ...), kind=kOutput, calls=%fused_computation.82.clone.1 | convolution fusion | flops 1622671360 | bytes 8486944 | tf_op jit(solution)/shard_map/while/body/tab,taf->tbf/dot_general | solution.py:49
  401.4 2.8 gather_fusion.4
  404.2 9.7 %fusion.142 = f32[32,128,256]{2,1,0:T(8,128)S(1)} fusion(f32[32,128,256]{2,1,0:T(8,128)} %gather_fusion.4, s32[32,128]{1,0:T(8,128)S(1)} %get-tuple-element.407, s32[32,128]{1,0:T(8,128)S(1)} %get-tuple-element.409, s32[32,128]{1,0:T(8,128)S(1)} %get-tuple-element.410, s32[32,128]{1,0:T(8,128)S(1)} %get-tuple-element.411, ...), kind=kOutput, calls=%fused_computation.82.clone.1 | convolution fusion | flops 1622671360 | bytes 8486944 | tf_op jit(solution)/shard_map/while/body/tab,taf->tbf/dot_general | solution.py:49
  422.7 2.8 gather_fusion.4
  425.5 9.7 %fusion.142 = f32[32,128,256]{2,1,0:T(8,128)S(1)} fusion(f32[32,128,256]{2,1,0:T(8,128)} %gather_fusion.4, s32[32,128]{1,0:T(8,128)S(1)} %get-tuple-element.407, s32[32,128]{1,0:T(8,128)S(1)} %get-tuple-element.409, s32[32,128]{1,0:T(8,128)S(1)} %get-tuple-element.410, s32[32,128]{1,0:T(8,128)S(1)} %get-tuple-element.411, ...), kind=kOutput, calls=%fused_computation.82.clone.1 | convolution fusion | flops 1622671360 | bytes 8486944 | tf_op jit(solution)/shard_map/while/body/tab,taf->tbf/dot_general | solution.py:49
  444.0 2.8 gather_fusion.4
  446.8 9.7 %fusion.142 = f32[32,128,256]{2,1,0:T(8,128)S(1)} fusion(f32[32,128,256]{2,1,0:T(8,128)} %gather_fusion.4, s32[32,128]{1,0:T(8,128)S(1)} %get-tuple-element.407, s32[32,128]{1,0:T(8,128)S(1)} %get-tuple-element.409, s32[32,128]{1,0:T(8,128)S(1)} %get-tuple-element.410, s32[32,128]{1,0:T(8,128)S(1)} %get-tuple-element.411, ...), kind=kOutput, calls=%fused_computation.82.clone.1 | convolution fusion | flops 1622671360 | bytes 8486944 | tf_op jit(solution)/shard_map/while/body/tab,taf->tbf/dot_general | solution.py:49
  465.3 2.8 gather_fusion.4
  468.1 9.7 %fusion.142 = f32[32,128,256]{2,1,0:T(8,128)S(1)} fusion(f32[32,128,256]{2,1,0:T(8,128)} %gather_fusion.4, s32[32,128]{1,0:T(8,128)S(1)} %get-tuple-element.407, s32[32,128]{1,0:T(8,128)S(1)} %get-tuple-element.409, s32[32,128]{1,0:T(8,128)S(1)} %get-tuple-element.410, s32[32,128]{1,0:T(8,128)S(1)} %get-tuple-element.411, ...), kind=kOutput, calls=%fused_computation.82.clone.1 | convolution fusion | flops 1622671360 | bytes 8486944 | tf_op jit(solution)/shard_map/while/body/tab,taf->tbf/dot_general | solution.py:49
  486.7 2.8 gather_fusion.4
  489.4 9.7 %fusion.142 = f32[32,128,256]{2,1,0:T(8,128)S(1)} fusion(f32[32,128,256]{2,1,0:T(8,128)} %gather_fusion.4, s32[32,128]{1,0:T(8,128)S(1)} %get-tuple-element.407, s32[32,128]{1,0:T(8,128)S(1)} %get-tuple-element.409, s32[32,128]{1,0:T(8,128)S(1)} %get-tuple-element.410, s32[32,128]{1,0:T(8,128)S(1)} %get-tuple-element.411, ...), kind=kOutput, calls=%fused_computation.82.clone.1 | convolution fusion | flops 1622671360 | bytes 8486944 | tf_op jit(solution)/shard_map/while/body/tab,taf->tbf/dot_general | solution.py:49
  508.0 2.8 gather_fusion.4
  510.8 9.7 %fusion.142 = f32[32,128,256]{2,1,0:T(8,128)S(1)} fusion(f32[32,128,256]{2,1,0:T(8,128)} %gather_fusion.4, s32[32,128]{1,0:T(8,128)S(1)} %get-tuple-element.407, s32[32,128]{1,0:T(8,128)S(1)} %get-tuple-element.409, s32[32,128]{1,0:T(8,128)S(1)} %get-tuple-element.410, s32[32,128]{1,0:T(8,128)S(1)} %get-tuple-element.411, ...), kind=kOutput, calls=%fused_computation.82.clone.1 | convolution fusion | flops 1622671360 | bytes 8486944 | tf_op jit(solution)/shard_map/while/body/tab,taf->tbf/dot_general | solution.py:49
  531.3 4.5 fusion.95
  535.8 14.4 %all-reduce.2.cloned.1.call-done = f32[256,2048]{0,1:T(8,128)} async-done(((f32[256,2048]{0,1:T(8,128)}), f32[256,2048]{0,1:T(8,128)}) %all-reduce.2.cloned.1.call-update) | async-done | bytes 2097168 | tf_op jit(solution)/shard_map/psum | solution.py:107
  550.2 2.9 copy.10
  553.0 17.9 %reduce-scatter.8.cloned.1.call-done = f32[128,256]{1,0:T(8,128)} async-done(((f32[1024,256]{1,0:T(8,128)}), f32[128,256]{1,0:T(8,128)}) %reduce-scatter.8.cloned.1.call-update) | async-done | bytes 131088 | tf_op jit(solution)/shard_map/reduce_scatter | solution.py:94
  (298 shorter events, 142.5 us)
Async XLA Ops:
  8.0 215.4 %reduce-scatter.4.cloned.1.call-start = ((), (), s32[]{:S(2)}) async-start(), calls=%async_computation.3 | async-start | bytes 2621440 | tf_op jit(solution)/shard_map/reduce_scatter | solution.py:83
  10.6 1.5 copy-start.8
  27.0 2.5 copy-start.3
  32.2 1.3 copy-start.4
  48.4 2.5 copy-start.3
  53.5 1.3 copy-start.4
  69.8 2.5 copy-start.3
  74.9 1.3 copy-start.4
  91.1 2.5 copy-start.3
  96.3 1.3 copy-start.4
  112.5 2.5 copy-start.3
  117.7 1.3 copy-start.4
  133.9 2.5 copy-start.3
  139.0 1.3 copy-start.4
  155.3 2.5 copy-start.3
  160.4 1.3 copy-start.4
  176.6 2.5 copy-start.3
  181.8 1.3 copy-start.4
  185.9 37.7 %all-gather.6.cloned.1.call-start = ((), (), s32[]{:S(2)}) async-start(), calls=%async_computation.5 | async-start | bytes 1179648 | tf_op jit(solution)/shard_map/all_gather | solution.py:84
  186.4 82.7 %all-gather.4.cloned.1.call-start = ((), (), s32[]{:S(2)}) async-start(), calls=%async_computation.4 | async-start | bytes 2621440 | tf_op jit(solution)/shard_map/all_gather | solution.py:85
  223.4 50.2 %copy-start.7 = (f32[512,256]{1,0:T(8,128)S(1)}, f32[512,256]{1,0:T(8,128)}, u32[]{:S(2)}) copy-start(f32[512,256]{1,0:T(8,128)} %param.13) | copy-start | bytes 1572868
  223.5 95.9 %reduce-scatter.6.cloned.1.call-start = ((), (), s32[]{:S(2)}) async-start(), calls=%async_computation.6 | async-start | bytes 2621440 | tf_op jit(solution)/shard_map/reduce_scatter | solution.py:90
  223.5 50.1 %copy-start.6 = (f32[1024,256]{1,0:T(8,128)S(1)}, f32[1024,256]{1,0:T(8,128)}, u32[]{:S(2)}) copy-start(f32[1024,256]{1,0:T(8,128)} %all-gather.6.cloned.1.call-done) | copy-start | bytes 3145732
  277.0 77.1 %all-gather.8.cloned.1.call-start = ((), (), s32[]{:S(2)}) async-start(), calls=%async_computation.7 | async-start | bytes 2621440 | tf_op jit(solution)/shard_map/all_gather | solution.py:95
  319.4 230.8 %all-reduce.2.cloned.1.call-start = ((), (), s32[]{:S(2)}) async-start(), calls=%async_computation.8 | async-start | bytes 4194304 | tf_op jit(solution)/shard_map/psum | solution.py:107
  354.1 2.3 copy-start
  371.3 2.5 copy-start.1
  376.4 1.3 copy-start.2
  392.6 2.5 copy-start.1
  397.7 1.3 copy-start.2
  413.9 2.5 copy-start.1
  419.1 1.3 copy-start.2
  435.2 2.5 copy-start.1
  440.4 1.3 copy-start.2
  456.5 2.5 copy-start.1
  461.7 1.3 copy-start.2
  477.9 2.5 copy-start.1
  483.0 1.3 copy-start.2
  499.2 2.5 copy-start.1
  504.3 1.3 copy-start.2
  520.5 2.5 copy-start.1
  525.6 1.3 copy-start.2
  529.7 1.6 copy-start.5
  529.7 41.2 %reduce-scatter.8.cloned.1.call-start = ((), (), s32[]{:S(2)}) async-start(), calls=%async_computation.9 | async-start | bytes 1179648 | tf_op jit(solution)/shard_map/reduce_scatter | solution.py:94
Sparse Core Ops, SparseCore 0:
  186.0 37.4 reduce-scatter.3
  319.5 34.5 all-gather.7
  529.8 20.3 all-reduce.1
Sparse Core Ops, SparseCore 1:
  188.2 27.7 all-gather.5
  223.5 45.5 all-gather.3
  277.0 42.3 reduce-scatter.5
  535.9 35.0 reduce-scatter.7
where the time goes:
time: 581 us; the launch traced here: 578 us
  matrix products  211 us (36%)
  waiting for transfers between devices  192 us (33%)
  local copies, waits for them, and re-layouts  143 us (25%)
  between operations  16.2 us (3%)
  other arithmetic  13.7 us (2%)
    dot_general x8, matrix products, advance(): jnp.einsum('tab,tbf->taf', values, source[col_picks], precision=highest)  78.2 us
    dot_general x8, matrix products, advance(): jnp.einsum('tab,taf->tbf', values, source[row_picks], precision=highest)  77.8 us
    while x80, local copies, waits for them, and re-layouts  60 us
    all_gather x1, waiting for transfers between devices, per_device(): hidden_all = lax.all_gather(hidden, 'feat', axis=1, tiled=True)  45.6 us
    dot_general x16, matrix products, advance(): jnp.dot(placing, product.reshape(tile_batch, tile * width), precision=hig...  43 us
    reduce_scatter x1, waiting for transfers between devices, per_device(): lax.psum_scatter(jnp.dot(grad_pre, weight_cols.T, precision=highest), 'fe...  42.4 us
    reduce_scatter x1, waiting for transfers between devices, per_device(): lax.psum_scatter(partial_value, 'nbr', scatter_dimension=0, tiled=True)  36.9 us
    all_gather x1, waiting for transfers between devices, per_device(): grad_block = lax.all_gather(grad_hidden, 'nbr', axis=0, tiled=True)  34.4 us
  transfers between devices with their start and end apart: 7, of which 6 were waited for; matrix products, arithmetic and copies ran while one was open for 1% of the time, Pallas kernels for 0%

commit v1 on v0

v1 whole, which is shorter than its diff:
```python
import functools

import jax
import jax.numpy as jnp
from jax import lax
from jax.experimental import pallas as pl
from jax.experimental.pallas import tpu as pltpu
from jax.sharding import PartitionSpec as P

TILE = 128
modulus = 32749
high = lax.Precision.HIGH
BF16, F32, I32 = jnp.bfloat16, jnp.float32, jnp.int32
VMEM_BYTES = 56 * 1024 * 1024


def mod_p(value):
    quotient = (value.astype(F32) * (1.0 / modulus)).astype(I32)
    rest = value - quotient * modulus
    rest = jnp.where(rest < 0, rest + modulus, rest)
    return jnp.where(rest >= modulus, rest - modulus, rest)


def halves(value):
    upper = value.astype(BF16)
    return upper, (value - upper.astype(F32)).astype(BF16)


def dot(a, b):
    return jnp.dot(a, b, preferred_element_type=F32)


def dot3(a_hi, a_lo, b_hi, b_lo):
    return dot(a_hi, b_hi) + (dot(a_hi, b_lo) + dot(a_lo, b_hi))


def edge_setup(row_id, nbr_id, pairs, total, row_part, col_part, inner, occupied):
    r_dev, c_dev = row_part.shape[0], inner.shape[1]
    row_blocks = r_dev // TILE
    slots = pairs.shape[1]
    r = row_id * r_dev + lax.broadcasted_iota(I32, (r_dev, TILE), 0)
    row_part[...] = mod_p(3 * r * r + 11 * r).astype(F32) - 1.5 * modulus
    c = nbr_id * c_dev + lax.broadcasted_iota(I32, (row_blocks, c_dev), 1)
    first = row_id * r_dev + TILE * lax.broadcasted_iota(I32, (row_blocks, c_dev), 0)
    columns = mod_p(5 * mod_p(c * c) + 13 * c + 7 * mod_p(first * c)).astype(F32)
    c = nbr_id * c_dev + lax.broadcasted_iota(I32, (TILE, c_dev), 1)
    i = lax.broadcasted_iota(I32, (TILE, c_dev), 0)
    inner[...] = mod_p(7 * i * c).astype(F32)
    listed = lax.broadcasted_iota(I32, (row_blocks, slots), 1) < total
    named = lax.broadcasted_iota(I32, (row_blocks, slots), 0) == pairs[0:1, :]
    row_hot = jnp.where(named & listed, 1.0, 0.0).astype(BF16)
    blocks = lax.broadcasted_iota(I32, (c_dev, slots), 0) // TILE
    col_hot = jnp.where(blocks == pairs[1:2, :], 1.0, 0.0).astype(BF16)
    tiles = lax.dot_general(
        row_hot, col_hot, (((1,), (1,)), ((), ())), preferred_element_type=F32
    )
    for block in range(row_blocks):
        col_part[block] = columns[block : block + 1, :]
        occupied[block] = tiles[block : block + 1, :]


def edge_rows(block, col, tables):
    row_part, col_part, inner, occupied = tables
    rows = pl.ds(pl.multiple_of(block * TILE, TILE), TILE)
    cols = pl.ds(col * TILE, TILE)
    total = row_part[rows, :] + (inner[:, cols] + col_part[block, :, cols])
    shift = jnp.where(
        total >= 0.5 * modulus, -1.0 * modulus, jnp.where(total < -0.5 * modulus, 1.0 * modulus, 0.0)
    )
    return halves((total + shift) * occupied[block, :, cols])


def fill(slot_hi, slot_lo, block, offset, tables):
    for col in range(slot_hi.shape[1] // TILE):
        upper, lower = edge_rows(block, col, tables)
        slot_hi[offset : offset + TILE, col * TILE : (col + 1) * TILE] = upper
        slot_lo[offset : offset + TILE, col * TILE : (col + 1) * TILE] = lower


def table_shapes(r_dev, c_dev):
    blocks = r_dev // TILE
    return [
        pltpu.VMEM((r_dev, TILE), F32),
        pltpu.VMEM((blocks, 1, c_dev), F32),
        pltpu.VMEM((TILE, c_dev), F32),
        pltpu.VMEM((blocks, 1, c_dev), F32),
    ]


def forward_kernel(scale, ids, total, pairs, x, out, x_hi, x_lo, a_hi, a_lo, *tables):
    edge_setup(ids[0], ids[1], pairs, total[0], *tables)
    upper, lower = halves(x[...].T)
    x_hi[...] = upper
    x_lo[...] = lower
    step = a_hi.shape[0]

    def advance(chunk, carry):
        for part in range(step // TILE):
            fill(a_hi, a_lo, chunk * (step // TILE) + part, part * TILE, tables)
        rows = pl.ds(pl.multiple_of(chunk * step, step), step)
        out[rows, :] = scale * dot3(a_hi[...], a_lo[...], x_hi[...], x_lo[...])
        return carry

    lax.fori_loop(0, out.shape[0] // step, advance, 0)


def backward_kernel(scale, ids, total, pairs, grad, out, a_hi, a_lo, *tables):
    edge_setup(ids[0], ids[1], pairs, total[0], *tables)
    step = a_hi.shape[0]
    out[...] = jnp.zeros_like(out)

    def advance(chunk, carry):
        for part in range(step // TILE):
            fill(a_hi, a_lo, chunk * (step // TILE) + part, part * TILE, tables)
        rows = pl.ds(pl.multiple_of(chunk * step, step), step)
        g_hi, g_lo = halves(grad[rows, :].T * scale)
        out[...] += dot3(g_hi, g_lo, a_hi[...], a_lo[...])
        return carry

    lax.fori_loop(0, grad.shape[0] // step, advance, 0)


def local_call(kernel, out_shape, scratch, args, flops):
    smem = pl.BlockSpec(memory_space=pltpu.SMEM)
    vmem = pl.BlockSpec(memory_space=pltpu.VMEM)
    return pl.pallas_call(
        kernel,
        out_shape=jax.ShapeDtypeStruct(out_shape, F32),
        in_specs=[smem, smem, vmem, vmem],
        out_specs=vmem,
        scratch_shapes=scratch,
        compiler_params=pltpu.CompilerParams(vmem_limit_bytes=VMEM_BYTES),
        cost_estimate=pl.CostEstimate(flops=flops, bytes_accessed=4 << 20, transcendentals=0),
    )(*args)


def per_device(features, tile_list, tile_count, weight, cotangent):
    pairs = tile_list[0, 0]
    n_nbr = lax.axis_size("nbr")
    width, c_dev = features.shape
    r_dev = cotangent.shape[0] * n_nbr
    scale = (12.0 / (c_dev * n_nbr / 2)) ** 0.5 / modulus
    ids = jnp.stack([lax.axis_index("row"), lax.axis_index("nbr")]).astype(I32)
    total = tile_count[0]
    tables = table_shapes(r_dev, c_dev)
    flops = 6 * r_dev * c_dev * width
    adjacency = [pltpu.VMEM((256, c_dev), BF16)] * 2
    partial_value = local_call(
        functools.partial(forward_kernel, scale),
        (r_dev, width),
        [pltpu.VMEM((c_dev, width), BF16)] * 2 + adjacency + tables,
        (ids, total, pairs, features),
        flops,
    )
    hidden = lax.psum_scatter(partial_value, "nbr", scatter_dimension=0, tiled=True)
    weight_cols = lax.all_gather(weight, ("row", "nbr"), axis=0, tiled=True)
    hidden_all = lax.all_gather(hidden, "feat", axis=1, tiled=True)
    pre_act = jnp.dot(hidden_all, weight_cols, precision=high)
    squash = jax.nn.sigmoid(pre_act)
    activations = pre_act * squash
    grad_pre = cotangent * squash * (1.0 + pre_act * (1.0 - squash))
    grad_hidden = lax.psum_scatter(
        jnp.dot(grad_pre, weight_cols.T, precision=high), "feat", scatter_dimension=1, tiled=True
    )
    weight_terms = jnp.dot(hidden_all.T, grad_pre, precision=high)
    weight_grad = lax.psum_scatter(weight_terms, ("row", "nbr"), scatter_dimension=0, tiled=True)
    grad_block = lax.all_gather(grad_hidden, "nbr", axis=0, tiled=True)
    column_part = local_call(
        functools.partial(backward_kernel, scale),
        (width, c_dev),
        adjacency + tables,
        (ids, total, pairs, grad_block),
        flops,
    )
    feature_grad = lax.psum(column_part, "row")
    return (activations, feature_grad, weight_grad)


def solution(mesh):
    in_specs = (
        P("feat", "nbr"),
        P("row", "nbr", None, None),
        P("row", "nbr"),
        P(("row", "nbr"), "feat"),
        P(("row", "nbr"), "feat"),
    )
    out_specs = (P(("row", "nbr"), "feat"), P("feat", "nbr"), P(("row", "nbr"), "feat"))
    return jax.shard_map(
        per_device, mesh=mesh, in_specs=in_specs, out_specs=out_specs, check_vma=False
    )
```

time: 581 us -> 248 us (0.43)
  matrix products: 211 us -> 8.97 us
  local copies, waits for them, and re-layouts: 143 us -> 3.15 us
  Pallas kernels: 0 us -> 37.6 us
  other arithmetic: 13.7 us -> 0.61 us
  waiting for transfers between devices: 192 us -> 181 us
    dot_general x35 -> x3, matrix products: 211 us -> 8.97 us  [the longest x1 3.68 us: per_device(): pre_act = jnp.dot(hidden_all, weight_cols, precision=high)]
    gather x48 -> x0, local copies, waits for them, and re-layouts: 67.1 us -> none  [the longest x8 22.2 us: advance(): source[row_picks]]
    while x80 -> x0, local copies, waits for them, and re-layouts: 60 us -> none
    pallas_call x0 -> x2, Pallas kernels: none -> 37.6 us  [local_call(): pl.pallas_call(kernel, out_shape=jax.ShapeDtypeStruct(out_shape, F32), in...]
    reduce_scatter x1, waiting for transfers between devices: 17.9 us -> 0.03 us  [per_device(): lax.psum_scatter(weight_terms, ('row', 'nbr'), scatter_dimension=0, tiled...]
    lt x16 -> x0, other arithmetic: 10.4 us -> none  [advance(): in_range = positions < end_slot]
    psum x1, waiting for transfers between devices: 14.4 us -> 21.3 us  [per_device(): feature_grad = lax.psum(column_part, 'row')]
  transfers between devices with their start and end apart: 7 -> 7, of which waited for: 6 -> 5; matrix products, arithmetic and copies ran while one was open for 1% -> 1% of each run, Pallas kernels for 0% -> 8%
where the time goes in v1:
time: 248 us; the launch traced here: 247 us
  waiting for transfers between devices  181 us (73%)
  Pallas kernels  37.6 us (15%)
  between operations  16.2 us (7%)
  matrix products  8.97 us (4%)
  local copies, waits for them, and re-layouts  3.15 us (1%)
    all_gather x1, waiting for transfers between devices, per_device(): hidden_all = lax.all_gather(hidden, 'feat', axis=1, tiled=True)  45.6 us
    reduce_scatter x1, waiting for transfers between devices, per_device(): lax.psum_scatter(jnp.dot(grad_pre, weight_cols.T, precision=high), 'feat'...  42.3 us
    reduce_scatter x1, waiting for transfers between devices, per_device(): lax.psum_scatter(partial_value, 'nbr', scatter_dimension=0, tiled=True)  38.8 us
    pallas_call x2, Pallas kernels, local_call(): pl.pallas_call(kernel, out_shape=jax.ShapeDtypeStruct(out_shape, F32), in...  37.6 us
    all_gather x1, waiting for transfers between devices, per_device(): grad_block = lax.all_gather(grad_hidden, 'nbr', axis=0, tiled=True)  32 us
    psum x1, waiting for transfers between devices, per_device(): feature_grad = lax.psum(column_part, 'row')  21.3 us
  transfers between devices with their start and end apart: 7, of which 5 were waited for; matrix products, arithmetic and copies ran while one was open for 1% of the time, Pallas kernels for 8%

profile of v1, /device:TPU:0, one launch (start us, length us, event | category | flops | bytes accessed | tf_op | source)
XLA Modules:
  0.0 247.5 jit_solution(12454014711989306935)
XLA Ops:
  8.0 0.0 reduce-scatter.4.cloned.1.call-start
  8.7 0.6 pad_add_fusion.ids
  9.3 18.0 %shard_map.76 = f32[2048,256]{1,0:T(8,128)} custom-call(s32[2]{0:T(128)} %pad_add_fusion.ids, s32[1]{0:T(128)} %bitcast.8.total, s32[2,256]{1,0:T(2,128)} %bitcast.10, f32[256,2048]{1,0:T(8,128)} %x.1), custom_call_target="tpu_custom_call" | custom-call | flops 6442450944 | bytes 4194304 | tf_op jit(solution)/shard_map/pallas_call | solution.py:126
  27.3 0.0 reduce-scatter.4.cloned.1.call-update
  27.3 0.0 all-gather.6.cloned.1.call-start
  27.4 0.5 all-gather.6.cloned.1.call-update
  27.9 0.0 all-gather.4.cloned.1.call-start
  28.0 38.8 %reduce-scatter.4.cloned.1.call-done = f32[512,256]{1,0:T(8,128)} async-done(((f32[2048,256]{1,0:T(8,128)}), f32[512,256]{1,0:T(8,128)}) %reduce-scatter.4.cloned.1.call-update) | async-done | bytes 524304 | tf_op jit(solution)/shard_map/reduce_scatter | solution.py:155
  66.8 0.0 all-gather.4.cloned.1.call-update
  66.8 0.0 copy-start.2
  66.8 0.0 reduce-scatter.6.cloned.1.call-start
  66.9 0.0 all-gather.6.cloned.1.call-done
  66.9 0.0 copy-start.1
  66.9 45.6 %all-gather.4.cloned.1.call-done = f32[512,1024]{1,0:T(8,128)} async-done(((f32[512,256]{1,0:T(8,128)}), f32[512,1024]{1,0:T(8,128)}) %all-gather.4.cloned.1.call-update) | async-done | bytes 2097168 | tf_op jit(solution)/shard_map/all_gather | solution.py:157
  112.5 3.7 %fusion = (f32[512,256]{1,0:T(8,128)}, f32[512,256]{1,0:T(8,128)S(1)}) fusion(f32[512,1024]{1,0:T(8,128)} %all-gather.4.cloned.1.call-done, f32[1024,256]{1,0:T(8,128)} %all-gather.6.cloned.1.call-done), kind=kOutput, calls=%fused_computation.2 | convolution fusion | flops 805830656 | bytes 4194304 | tf_op jit(solution)/shard_map/dot_general | solution.py:158
  116.2 0.0 copy-done.2
  116.2 0.0 copy-done.1
  116.2 2.5 %fusion.2 = f32[512,1024]{1,0:T(8,128)} fusion(f32[1024,256]{1,0:T(8,128)S(1)} %copy-done.1, f32[512,256]{1,0:T(8,128)S(1)} %get-tuple-element.4, f32[512,256]{1,0:T(8,128)S(1)} %copy-done.2), kind=kOutput, calls=%fused_computation.5 | convolution fusion | flops 806354944 | bytes 4194304 | tf_op jit(solution)/shard_map/dot_general | solution.py:163
  118.7 0.0 copy-start
  118.7 0.0 reduce-scatter.6.cloned.1.call-update
  118.7 0.0 all-gather.8.cloned.1.call-start
  118.7 42.3 %reduce-scatter.6.cloned.1.call-done = f32[512,256]{1,0:T(8,128)} async-done(((f32[512,1024]{1,0:T(8,128)}), f32[512,256]{1,0:T(8,128)}) %reduce-scatter.6.cloned.1.call-update) | async-done | bytes 524304 | tf_op jit(solution)/shard_map/reduce_scatter | solution.py:162
  161.1 0.0 all-gather.8.cloned.1.call-update
  161.1 0.0 reduce-scatter.8.cloned.1.call-start
  161.2 0.0 copy-done
  161.2 2.8 %fusion.1 = f32[1024,256]{1,0:T(8,128)} fusion(f32[512,1024]{1,0:T(8,128)S(1)} %copy-done, f32[512,256]{1,0:T(8,128)S(1)} %get-tuple-element.4, f32[512,256]{1,0:T(8,128)S(1)} %copy-done.2), kind=kOutput, calls=%fused_computation.4 | convolution fusion | flops 806354944 | bytes 4194304 | tf_op jit(solution)/shard_map/dot_general | solution.py:165
  164.0 0.0 reduce-scatter.8.cloned.1.call-update
  164.0 0.0 all-reduce.2.cloned.1.call-start
  164.0 32.0 %all-gather.8.cloned.1.call-done.grad = f32[2048,256]{1,0:T(8,128)} async-done(((f32[512,256]{1,0:T(8,128)}), f32[2048,256]{1,0:T(8,128)}) %all-gather.8.cloned.1.call-update) | async-done | bytes 2097168 | tf_op jit(solution)/shard_map/all_gather | solution.py:167
  196.0 19.6 %shard_map.77 = f32[256,2048]{1,0:T(8,128)} custom-call(s32[2]{0:T(128)} %pad_add_fusion.ids, s32[1]{0:T(128)} %bitcast.9.total, s32[2,256]{1,0:T(2,128)} %bitcast.11, f32[2048,256]{1,0:T(8,128)} %all-gather.8.cloned.1.call-done.grad), custom_call_target="tpu_custom_call" | custom-call | flops 6442450944 | bytes 4194304 | tf_op jit(solution)/shard_map/pallas_call | solution.py:126
  215.6 0.0 all-reduce.2.cloned.1.call-update
  215.6 0.0 reduce-scatter.8.cloned.1.call-done
  215.7 21.3 %all-reduce.2.cloned.1.call-done = f32[256,2048]{1,0:T(8,128)} async-done(((f32[256,2048]{1,0:T(8,128)}), f32[256,2048]{1,0:T(8,128)}) %all-reduce.2.cloned.1.call-update) | async-done | bytes 2097168 | tf_op jit(solution)/shard_map/psum | solution.py:175
  237.0 3.1 %copy.10 = f32[256,2048]{1,0:T(8,128)} copy(f32[256,2048]{1,0:T(8,128)} %all-reduce.2.cloned.1.call-done) | data formatting | bytes 4194304
Async XLA Ops:
  8.0 58.8 %reduce-scatter.4.cloned.1.call-start = ((), (), s32[]{:S(2)}) async-start(), calls=%async_computation.3 | async-start | bytes 2621440 | tf_op jit(solution)/shard_map/reduce_scatter | solution.py:155
  27.3 39.5 %all-gather.6.cloned.1.call-start = ((), (), s32[]{:S(2)}) async-start(), calls=%async_computation.5 | async-start | bytes 1179648 | tf_op jit(solution)/shard_map/all_gather | solution.py:156
  27.9 84.6 %all-gather.4.cloned.1.call-start = ((), (), s32[]{:S(2)}) async-start(), calls=%async_computation.4 | async-start | bytes 2621440 | tf_op jit(solution)/shard_map/all_gather | solution.py:157
  66.8 49.4 %copy-start.2 = (f32[512,256]{1,0:T(8,128)S(1)}, f32[512,256]{1,0:T(8,128)}, u32[]{:S(2)}) copy-start(f32[512,256]{1,0:T(8,128)} %param.9) | copy-start | bytes 1572868
  66.8 94.3 %reduce-scatter.6.cloned.1.call-start = ((), (), s32[]{:S(2)}) async-start(), calls=%async_computation.6 | async-start | bytes 2621440 | tf_op jit(solution)/shard_map/reduce_scatter | solution.py:162
  66.9 49.3 %copy-start.1 = (f32[1024,256]{1,0:T(8,128)S(1)}, f32[1024,256]{1,0:T(8,128)}, u32[]{:S(2)}) copy-start(f32[1024,256]{1,0:T(8,128)} %all-gather.6.cloned.1.call-done) | copy-start | bytes 3145732
  118.7 42.5 %copy-start = (f32[512,1024]{1,0:T(8,128)S(1)}, f32[512,1024]{1,0:T(8,128)}, u32[]{:S(2)}) copy-start(f32[512,1024]{1,0:T(8,128)} %all-gather.4.cloned.1.call-done) | copy-start | bytes 6291460
  118.7 77.3 %all-gather.8.cloned.1.call-start = ((), (), s32[]{:S(2)}) async-start(), calls=%async_computation.7 | async-start | bytes 2621440 | tf_op jit(solution)/shard_map/all_gather | solution.py:167
  161.1 54.6 %reduce-scatter.8.cloned.1.call-start = ((), (), s32[]{:S(2)}) async-start(), calls=%async_computation.9 | async-start | bytes 1179648 | tf_op jit(solution)/shard_map/reduce_scatter | solution.py:166
  164.0 73.0 %all-reduce.2.cloned.1.call-start = ((), (), s32[]{:S(2)}) async-start(), calls=%async_computation.8 | async-start | bytes 4194304 | tf_op jit(solution)/shard_map/psum | solution.py:175
Sparse Core Ops, SparseCore 0:
  27.5 39.2 reduce-scatter.3
  161.2 34.7 all-gather.7
  215.8 21.2 all-reduce.1
Sparse Core Ops, SparseCore 1:
  29.7 29.6 all-gather.5
  66.9 45.5 all-gather.3
  118.8 42.3 reduce-scatter.5
  166.0 43.2 reduce-scatter.7

commit v2 on v1

--- a/solution.py
+++ b/solution.py
@@ -134,6 +134,381 @@
     )(*args)
 
 
+MESH = pl.DeviceIdType.MESH
+CHUNKS = 4
+
+
+def fused_kernel(
+    scale, total, pairs, x, w, cot,
+    act, own_out, other_out, wg_out,
+    x_hi, x_lo, a_hi, a_lo, part, dx, dy, rx, ry, h, h_hi, h_lo, gp, rl, rr, ga,
+    wall, w_hi, w_lo, wt_hi, wt_lo, wterm, wpeer, wsum, wrecv,
+    d_s, d_r, p_s, p_r, ag_s, ag_r, rs_s, rs_r, t_s, t_r,
+    w_s, w_r, wp_s, wp_r, wg_s, wg_r, out_s, out_r, *tables,
+):
+    row, n, z = lax.axis_index("row"), lax.axis_index("nbr"), lax.axis_index("feat")
+    col, line = lax.rem(n, 2), n // 2
+    nx, ny, nd = line * 2 + (1 - col), (1 - line) * 2 + col, 3 - n
+    peer = 1 - row
+    right, left = jnp.minimum(z + 1, 3), jnp.maximum(z - 1, 0)
+    half = TILE // 2
+    owners = (nd, nx, ny, n)
+
+    def send(src, dst, s_sem, r_sem, **to):
+        return pltpu.make_async_remote_copy(
+            src_ref=src, dst_ref=dst, send_sem=s_sem, recv_sem=r_sem,
+            device_id=to, device_id_type=MESH,
+        )
+
+    def copy_diag(k, way):
+        rows = pl.ds(way * half, half)
+        return send(part.at[k, 0, rows], (dx, dy)[way].at[k], d_s.at[k, way], d_r.at[k, way],
+                    nbr=(nx, ny)[way])
+
+    def copy_part(k, way):
+        return send(part.at[k, 1 + way], (rx, ry)[way].at[k], p_s.at[k, way], p_r.at[k, way],
+                    nbr=(nx, ny)[way])
+
+    def copy_hidden(k, block, step, way):
+        return send(h.at[k, block], h.at[k, block], ag_s.at[k, way * 3 + step], ag_r.at[k, block],
+                    feat=(right, left)[way])
+
+    def copy_sum(k, block, step, way):
+        buffer = (rl, rr)[way]
+        return send(buffer.at[k, block], buffer.at[k, block], rs_s.at[k, way * 3 + step],
+                    rs_r.at[k, way * 4 + block], feat=(right, left)[way])
+
+    def copy_grad(k, way):
+        return send(ga.at[k, 3], ga.at[k, 1 + way], t_s.at[k, way], t_r.at[k, way], nbr=(nx, ny)[way])
+
+    def copy_on(k, way):
+        rows = pl.ds(way * half, half)
+        return send(ga.at[k, 1 + way, rows], ga.at[k, 0, rows], t_s.at[k, 2 + way], t_r.at[k, 2 + way],
+                    nbr=(ny, nx)[way])
+
+    def copy_weight(j, source):
+        return send(w, wall.at[row * 4 + source], w_s.at[j], w_r.at[source], nbr=owners[j])
+
+    def copy_weight_peer(m, side):
+        return send(wall.at[side * 4 + m], wall.at[side * 4 + m], wp_s.at[m], wp_r.at[m], row=peer)
+
+    def copy_terms():
+        return send(wterm.at[pl.ds(peer * 4, 4)], wpeer, wg_s.at[3], wg_r.at[4], row=peer)
+
+    def copy_wsum(j, source):
+        return send(wsum.at[owners[j]], wrecv.at[source], wg_s.at[j], wg_r.at[source], nbr=owners[j])
+
+    piece = own_out.shape[1] // 4
+
+    def copy_out(j):
+        cols = pl.ds(j * piece, piece)
+        return send(own_out.at[:, cols], other_out.at[:, cols], out_s.at[j], out_r.at[j], row=peer)
+
+    barrier = pltpu.get_barrier_semaphore()
+    for target in (nx, ny, nd):
+        pl.semaphore_signal(barrier, inc=1, device_id={"nbr": target}, device_id_type=MESH)
+    pl.semaphore_signal(barrier, inc=1, device_id={"row": peer}, device_id_type=MESH)
+
+    @pl.when(z > 0)
+    def _():
+        pl.semaphore_signal(barrier, inc=1, device_id={"feat": left}, device_id_type=MESH)
+
+    @pl.when(z < 3)
+    def _():
+        pl.semaphore_signal(barrier, inc=1, device_id={"feat": right}, device_id_type=MESH)
+
+    edge_setup(row, n, pairs, total[0], *tables)
+    upper, lower = halves(x[...].T)
+    x_hi[...] = upper
+    x_lo[...] = lower
+    wall[row * 4 + n] = w[...]
+    wterm[...] = jnp.zeros_like(wterm)
+    own_out[...] = jnp.zeros_like(own_out)
+    pl.semaphore_wait(barrier, 4 + jnp.where(z > 0, 1, 0) + jnp.where(z < 3, 1, 0))
+    for j in range(3):
+        copy_weight(j, n).start()
+
+    def product(k, side):
+        for slot in (2 * side, 2 * side + 1):
+            fill(a_hi.at[k], a_lo.at[k], owners[slot] * CHUNKS + k, slot * TILE, tables)
+        rows = pl.ds(2 * side * TILE, 2 * TILE)
+        value = dot3(a_hi[k, rows, :], a_lo[k, rows, :], x_hi[...], x_lo[...])
+        part[k, 2 * side] = value[:TILE]
+        part[k, 2 * side + 1] = value[TILE:]
+
+    def gather_step(k, step):
+        @pl.when(z >= step)
+        def _():
+            copy_hidden(k, z - step, 0, 0).wait_recv()
+            if step < 3:
+                @pl.when(z < 3)
+                def _():
+                    copy_hidden(k, z - step, step, 0).start()
+
+        @pl.when(z <= 3 - step)
+        def _():
+            copy_hidden(k, z + step, 0, 1).wait_recv()
+            if step < 3:
+                @pl.when(z > 0)
+                def _():
+                    copy_hidden(k, z + step, step, 1).start()
+
+    def sum_step(k, step):
+        @pl.when((z >= 1) & (z <= 2) & (z <= step))
+        def _():
+            block = 3 - step + z
+            copy_sum(k, block, 0, 0).wait_recv()
+            rl[k, block] += gp[block]
+            copy_sum(k, block, step - z, 0).start()
+
+        @pl.when((z >= 1) & (z <= 2) & (3 - z <= step))
+        def _():
+            block = step + z - 3
+            copy_sum(k, block, 0, 1).wait_recv()
+            rr[k, block] += gp[block]
+            copy_sum(k, block, step - 3 + z, 1).start()
+
+    def dense(k):
+        rows = pl.ds(pl.multiple_of(k * TILE, TILE), TILE)
+        wide = h_hi.shape[1] // 4
+        for block in range(4):
+            cols = slice(block * wide, (block + 1) * wide)
+            h_hi[:, cols], h_lo[:, cols] = halves(h[k, block])
+        pre = dot3(h_hi[...], h_lo[...], w_hi[...], w_lo[...])
+        squash = jax.nn.sigmoid(pre)
+        act[rows, :] = pre * squash
+        grad_pre = cot[rows, :] * squash * (1.0 + pre * (1.0 - squash))
+        g_hi, g_lo = halves(grad_pre)
+        terms = dot3(g_hi, g_lo, wt_hi[...], wt_lo[...])
+        for block in range(4):
+            gp[block] = terms[:, block * wide : (block + 1) * wide]
+
+        @pl.when(z == 0)
+        def _():
+            for step in range(3):
+                rl[k, 3 - step] = gp[3 - step]
+                copy_sum(k, 3 - step, step, 0).start()
+
+        @pl.when(z == 3)
+        def _():
+            for step in range(3):
+                rr[k, step] = gp[step]
+                copy_sum(k, step, step, 1).start()
+
+        g_hi, g_lo = halves(grad_pre.T)
+        terms = dot3(g_hi, g_lo, h_hi[...], h_lo[...])
+        for block in range(8):
+            wterm[block] += terms[:, block * TILE : (block + 1) * TILE]
+
+    def advance(turn, carry):
+        f, m, s, b = turn, turn - 1, turn - 2, turn - 3
+        do_f, do_m = turn < 4, (turn >= 1) & (turn < 5)
+        do_s, do_b = (turn >= 2) & (turn < 6), turn >= 3
+
+        @pl.when(do_f)
+        def _():
+            product(f, 0)
+            copy_diag(f, 0).start()
+            copy_diag(f, 1).start()
+
+        @pl.when(do_m)
+        def _():
+            gather_step(m, 1)
+
+        @pl.when(do_s)
+        def _():
+            sum_step(s, 1)
+
+        @pl.when(do_b)
+        def _():
+            for way in range(2):
+                copy_grad(b, way).wait_recv()
+                copy_on(b, way).start()
+
+        @pl.when(do_f)
+        def _():
+            product(f, 1)
+            for way in range(2):
+                copy_diag(f, way).wait_recv()
+            part[f, 1, half:, :] += dy[f]
+            copy_part(f, 0).start()
+            part[f, 2, :half, :] += dx[f]
+            copy_part(f, 1).start()
+
+        @pl.when(do_m)
+        def _():
+            gather_step(m, 2)
+
+        @pl.when(do_s)
+        def _():
+            sum_step(s, 2)
+
+        @pl.when(turn == 0)
+        def _():
+            copy_weight_peer(n, row).start()
+            for j in range(3):
+                copy_weight(j, owners[j]).wait_recv()
+                copy_weight_peer(owners[j], row).start()
+
+        @pl.when(do_f)
+        def _():
+            for way in range(2):
+                copy_part(f, way).wait_recv()
+            h[f, z] = (part[f, 3] + rx[f] + ry[f]) * scale
+
+            @pl.when(z < 3)
+            def _():
+                copy_hidden(f, z, 0, 0).start()
+
+            @pl.when(z > 0)
+            def _():
+                copy_hidden(f, z, 0, 1).start()
+
+        @pl.when(turn == 0)
+        def _():
+            for m_ in range(4):
+                copy_weight_peer(m_, peer).wait_recv()
+            whole = wall[...].reshape(w_hi.shape)
+            w_hi[...], w_lo[...] = halves(whole)
+            wt_hi[...], wt_lo[...] = halves(whole.T)
+
+        @pl.when(do_s)
+        def _():
+            ga[s, 3] = gp[z]
+
+            @pl.when(z > 0)
+            def _():
+                copy_sum(s, z, 0, 0).wait_recv()
+                ga[s, 3] += rl[s, z]
+
+            @pl.when(z < 3)
+            def _():
+                copy_sum(s, z, 0, 1).wait_recv()
+                ga[s, 3] += rr[s, z]
+
+            for way in range(2):
+                copy_grad(s, way).start()
+
+        @pl.when(do_m)
+        def _():
+            gather_step(m, 3)
+            dense(m)
+
+        @pl.when(turn == 4)
+        def _():
+            copy_terms().start()
+
+        @pl.when(turn == 5)
+        def _():
+            copy_terms().wait_recv()
+            wsum[...] = wterm[pl.ds(row * 4, 4)] + wpeer[...]
+            for j in range(3):
+                copy_wsum(j, n).start()
+
+        @pl.when(do_b)
+        def _():
+            for way in range(2):
+                copy_on(b, way).wait_recv()
+            grads = ga[b].reshape(CHUNKS * TILE, ga.shape[3])
+            g_hi, g_lo = halves(grads.T * scale)
+            for j in range(4):
+                cols = slice(j * piece, (j + 1) * piece)
+                own_out[:, cols] += dot3(g_hi, g_lo, a_hi[b, :, cols], a_lo[b, :, cols])
+
+                @pl.when(turn == 6)
+                def _():
+                    copy_out(j).start()
+
+        return carry
+
+    lax.fori_loop(0, 7, advance, 0)
+
+    for j in range(3):
+        copy_wsum(j, owners[j]).wait_recv()
+    wg_out[...] = (wsum[n] + wrecv[nx] + wrecv[ny] + wrecv[nd]).T
+    for j in range(3):
+        copy_weight(j, n).wait_send()
+        copy_wsum(j, n).wait_send()
+    copy_terms().wait_send()
+    for m_ in range(4):
+        copy_weight_peer(m_, row).wait_send()
+
+    def settle(k, carry):
+        for way in range(2):
+            copy_diag(k, way).wait_send()
+            copy_part(k, way).wait_send()
+            copy_grad(k, way).wait_send()
+            copy_on(k, way).wait_send()
+        for step in range(3):
+            @pl.when((z >= step) & (z < 3))
+            def _():
+                copy_hidden(k, z - step, step, 0).wait_send()
+
+            @pl.when((z <= 3 - step) & (z > 0))
+            def _():
+                copy_hidden(k, z + step, step, 1).wait_send()
+
+            @pl.when(step < 3 - z)
+            def _():
+                copy_sum(k, 3, step, 0).wait_send()
+
+            @pl.when(step < z)
+            def _():
+                copy_sum(k, 0, step, 1).wait_send()
+        return carry
+
+    lax.fori_loop(0, CHUNKS, settle, 0)
+    for j in range(4):
+        copy_out(j).wait_send()
+        copy_out(j).wait_recv()
+
+
+def fused(features, pairs, total, weight, cotangent, scale):
+    width, c_dev = features.shape
+    full = 4 * width
+    r_dev = cotangent.shape[0] * 4
+    block = (CHUNKS, 4, TILE, width)
+    smem = pl.BlockSpec(memory_space=pltpu.SMEM)
+    vmem = pl.BlockSpec(memory_space=pltpu.VMEM)
+    dma = pltpu.SemaphoreType.DMA
+    scratch = [
+        pltpu.VMEM((c_dev, width), BF16), pltpu.VMEM((c_dev, width), BF16),
+        pltpu.VMEM((CHUNKS, 4 * TILE, c_dev), BF16), pltpu.VMEM((CHUNKS, 4 * TILE, c_dev), BF16),
+        pltpu.VMEM(block, F32),
+        pltpu.VMEM((CHUNKS, TILE // 2, width), F32), pltpu.VMEM((CHUNKS, TILE // 2, width), F32),
+        pltpu.VMEM((CHUNKS, TILE, width), F32), pltpu.VMEM((CHUNKS, TILE, width), F32),
+        pltpu.VMEM(block, F32),
+        pltpu.VMEM((TILE, full), BF16), pltpu.VMEM((TILE, full), BF16),
+        pltpu.VMEM(block[1:], F32),
+        pltpu.VMEM(block, F32), pltpu.VMEM(block, F32), pltpu.VMEM(block, F32),
+        pltpu.VMEM((8, full // 8, width), F32),
+        pltpu.VMEM((full, width), BF16), pltpu.VMEM((full, width), BF16),
+        pltpu.VMEM((width, full), BF16), pltpu.VMEM((width, full), BF16),
+        pltpu.VMEM((8, width, full // 8), F32),
+        pltpu.VMEM((4, width, full // 8), F32), pltpu.VMEM((4, width, full // 8), F32),
+        pltpu.VMEM((4, width, full // 8), F32),
+        dma((CHUNKS, 2)), dma((CHUNKS, 2)), dma((CHUNKS, 2)), dma((CHUNKS, 2)),
+        dma((CHUNKS, 6)), dma((CHUNKS, 4)), dma((CHUNKS, 6)), dma((CHUNKS, 8)),
+        dma((CHUNKS, 4)), dma((CHUNKS, 4)),
+        dma((3,)), dma((4,)), dma((4,)), dma((4,)), dma((4,)), dma((5,)), dma((4,)), dma((4,)),
+    ] + table_shapes(r_dev, c_dev)
+    shape = lambda *dims: jax.ShapeDtypeStruct(dims, F32)
+    act, own, other, wg = pl.pallas_call(
+        functools.partial(fused_kernel, scale),
+        out_shape=[shape(*cotangent.shape), shape(width, c_dev), shape(width, c_dev), shape(*weight.shape)],
+        in_specs=[smem, vmem, vmem, vmem, vmem],
+        out_specs=[vmem, vmem, pl.BlockSpec(memory_space=pl.ANY), vmem],
+        scratch_shapes=scratch,
+        compiler_params=pltpu.CompilerParams(
+            collective_id=0, has_side_effects=True, vmem_limit_bytes=VMEM_BYTES
+        ),
+        cost_estimate=pl.CostEstimate(
+            flops=12 * r_dev * c_dev * width, bytes_accessed=16 << 20, transcendentals=cotangent.size
+        ),
+    )(total, pairs, features, weight, cotangent)
+    return act, own + other, wg
+
+
 def per_device(features, tile_list, tile_count, weight, cotangent):
     pairs = tile_list[0, 0]
     n_nbr = lax.axis_size("nbr")
@@ -142,6 +517,9 @@
     scale = (12.0 / (c_dev * n_nbr / 2)) ** 0.5 / modulus
     ids = jnp.stack([lax.axis_index("row"), lax.axis_index("nbr")]).astype(I32)
     total = tile_count[0]
+    sizes = (lax.axis_size("row"), n_nbr, lax.axis_size("feat"))
+    if sizes == (2, 4, 4) and width % TILE == 0 and r_dev == 16 * TILE and weight.shape[0] == TILE:
+        return fused(features, pairs, total, weight, cotangent, scale)
     tables = table_shapes(r_dev, c_dev)
     flops = 6 * r_dev * c_dev * width
     adjacency = [pltpu.VMEM((256, c_dev), BF16)] * 2

time: 248 us -> 114 us (0.46)
  waiting for transfers between devices: 181 us -> 0 us
  Pallas kernels: 37.6 us -> 107 us
  between operations: 16.2 us -> 1.3 us
  matrix products: 8.97 us -> 0 us
  other arithmetic: 0.61 us -> 3.94 us
    reduce_scatter x3 -> x0, waiting for transfers between devices: 81.2 us -> none  [the longest x1 42.3 us: per_device(): lax.psum_scatter(jnp.dot(grad_pre, weight_cols.T, precision=high), 'feat'...]
    all_gather x3 -> x0, waiting for transfers between devices: 77.6 us -> none  [the longest x1 45.6 us: per_device(): hidden_all = lax.all_gather(hidden, 'feat', axis=1, tiled=True)]
    pallas_call x2 -> x1, Pallas kernels: 37.6 us -> 107 us  [fused(): pl.pallas_call(functools.partial(fused_kernel, scale), out_shape=[shape(*...]
    psum x1 -> x0, waiting for transfers between devices: 21.3 us -> none  [per_device(): feature_grad = lax.psum(column_part, 'row')]
    dot_general x3 -> x0, matrix products: 8.97 us -> none  [the longest x1 3.68 us: per_device(): pre_act = jnp.dot(hidden_all, weight_cols, precision=high)]
    add x0 -> x1, other arithmetic: none -> 3.94 us  [fused(): return (act, own + other, wg)]
  transfers between devices with their start and end apart: 7 -> 0, of which waited for: 5 -> 0; matrix products, arithmetic and copies ran while one was open for 1% -> 0% of each run, Pallas kernels for 8% -> 0%
where the time goes in v2:
time: 114 us
  Pallas kernels  107 us (94%)
  other arithmetic  3.94 us (3%)
  local copies, waits for them, and re-layouts  1.46 us (1%)
  between operations  1.3 us (1%)
    pallas_call x1, Pallas kernels, fused(): pl.pallas_call(functools.partial(fused_kernel, scale), out_shape=[shape(*...  107 us
    add x1, other arithmetic, fused(): return (act, own + other, wg)  3.94 us

profile of v2, /device:TPU:0, one launch (start us, length us, event | category | flops | bytes accessed | tf_op | source)
XLA Modules:
  0.0 113.8 jit_solution(14119184965911586409)
XLA Ops:
  1.3 107.1 %shard_map.76 = (f32[512,256]{1,0:T(8,128)}, f32[256,2048]{1,0:T(8,128)}, f32[256,2048]{1,0:T(8,128)}, f32[128,256]{1,0:T(8,128)}) custom-call(s32[1]{0:T(128)} %bitcast.2.total, s32[2,256]{1,0:T(2,128)} %bitcast.3, f32[256,2048]{1,0:T(8,128)} %x.1, f32[128,256]{1,0:T(8,128)} %w.1, f32[512,256]{1,0:T(8,128)} %cot.1), custom_call_target="tpu_custom_call" | custom-call | flops 12884901888 | bytes 16777216 | tf_op jit(solution)/shard_map/pallas_call | solution.py:496
  108.4 0.0 copy-start
  108.4 0.0 copy-start.1
  108.4 3.9 %add.3 = f32[256,2048]{1,0:T(8,128)} add(f32[256,2048]{1,0:T(8,128)} %get-tuple-element.8, f32[256,2048]{1,0:T(8,128)} %get-tuple-element.9) | non-fusion elementwise | flops 524288 | bytes 6291456 | tf_op jit(solution)/shard_map/add | solution.py:509
  112.4 0.0 copy-done
  112.4 0.8 copy.11
  113.2 0.0 copy-done.1
  113.2 0.7 copy.12
Async XLA Ops:
  108.4 4.0 %copy-start = (f32[512,256]{1,0:T(8,128)S(1)}, f32[512,256]{1,0:T(8,128)}, u32[]{:S(2)}) copy-start(f32[512,256]{1,0:T(8,128)} %get-tuple-element.14) | copy-start | bytes 1572868
  108.4 4.8 %copy-start.1 = (f32[128,256]{1,0:T(8,128)S(1)}, f32[128,256]{1,0:T(8,128)}, u32[]{:S(2)}) copy-start(f32[128,256]{1,0:T(8,128)} %get-tuple-element.16) | copy-start | bytes 393220

commit v3 on v2

--- a/solution.py
+++ b/solution.py
@@ -141,7 +141,7 @@
 def fused_kernel(
     scale, total, pairs, x, w, cot,
     act, own_out, other_out, wg_out,
-    x_hi, x_lo, a_hi, a_lo, part, dx, dy, rx, ry, h, h_hi, h_lo, gp, rl, rr, ga,
+    x_hi, x_lo, a_all, part, dx, dy, rx, ry, h, h_all, gp, rl, rr, ga,
     wall, w_hi, w_lo, wt_hi, wt_lo, wterm, wpeer, wsum, wrecv,
     d_s, d_r, p_s, p_r, ag_s, ag_r, rs_s, rs_r, t_s, t_r,
     w_s, w_r, wp_s, wp_r, wg_s, wg_r, out_s, out_r, *tables,
@@ -225,14 +225,15 @@
     wterm[...] = jnp.zeros_like(wterm)
     own_out[...] = jnp.zeros_like(own_out)
     pl.semaphore_wait(barrier, 4 + jnp.where(z > 0, 1, 0) + jnp.where(z < 3, 1, 0))
-    for j in range(3):
-        copy_weight(j, n).start()
 
     def product(k, side):
-        for slot in (2 * side, 2 * side + 1):
-            fill(a_hi.at[k], a_lo.at[k], owners[slot] * CHUNKS + k, slot * TILE, tables)
-        rows = pl.ds(2 * side * TILE, 2 * TILE)
-        value = dot3(a_hi[k, rows, :], a_lo[k, rows, :], x_hi[...], x_lo[...])
+        first = 4 * side * TILE
+        upper, lower = pl.ds(first, 2 * TILE), pl.ds(first + 2 * TILE, 2 * TILE)
+        for place in range(2):
+            block = owners[2 * side + place] * CHUNKS + k
+            fill(a_all.at[k, upper], a_all.at[k, lower], block, place * TILE, tables)
+        both = dot(a_all[k, pl.ds(first, 4 * TILE), :], x_hi[...])
+        value = both[: 2 * TILE] + (both[2 * TILE :] + dot(a_all[k, upper, :], x_lo[...]))
         part[k, 2 * side] = value[:TILE]
         part[k, 2 * side + 1] = value[TILE:]
 
@@ -270,16 +271,18 @@
 
     def dense(k):
         rows = pl.ds(pl.multiple_of(k * TILE, TILE), TILE)
-        wide = h_hi.shape[1] // 4
+        wide = h_all.shape[1] // 4
         for block in range(4):
             cols = slice(block * wide, (block + 1) * wide)
-            h_hi[:, cols], h_lo[:, cols] = halves(h[k, block])
-        pre = dot3(h_hi[...], h_lo[...], w_hi[...], w_lo[...])
+            h_all[:TILE, cols], h_all[TILE:, cols] = halves(h[k, block])
+        both = dot(h_all[...], w_hi[...])
+        pre = both[:TILE] + (both[TILE:] + dot(h_all[:TILE, :], w_lo[...]))
         squash = jax.nn.sigmoid(pre)
         act[rows, :] = pre * squash
         grad_pre = cot[rows, :] * squash * (1.0 + pre * (1.0 - squash))
         g_hi, g_lo = halves(grad_pre)
-        terms = dot3(g_hi, g_lo, wt_hi[...], wt_lo[...])
+        both = dot(jnp.concatenate([g_hi, g_lo], axis=0), wt_hi[...])
+        terms = both[:TILE] + (both[TILE:] + dot(g_hi, wt_lo[...]))
         for block in range(4):
             gp[block] = terms[:, block * wide : (block + 1) * wide]
 
@@ -296,34 +299,57 @@
                 copy_sum(k, step, step, 1).start()
 
         g_hi, g_lo = halves(grad_pre.T)
-        terms = dot3(g_hi, g_lo, h_hi[...], h_lo[...])
+        terms = dot(jnp.concatenate([g_hi, g_hi], axis=1), h_all[...]) + dot(g_lo, h_all[:TILE, :])
         for block in range(8):
             wterm[block] += terms[:, block * TILE : (block + 1) * TILE]
+
+    def back_product(k, last, pieces):
+        grads = ga[k].reshape(4 * TILE, ga.shape[3])
+        g_hi, g_lo = halves(grads.T * scale)
+        first, second = g_hi[:, : 2 * TILE], g_hi[:, 2 * TILE :]
+        doubled = jnp.concatenate([first, first, second, second], axis=1)
+        for j in pieces:
+            cols = slice(j * piece, (j + 1) * piece)
+            own_out[:, cols] += dot(doubled, a_all[k, :, cols]) + (
+                dot(g_lo[:, : 2 * TILE], a_all[k, : 2 * TILE, cols])
+                + dot(g_lo[:, 2 * TILE :], a_all[k, 4 * TILE : 6 * TILE, cols])
+            )
+
+            @pl.when(last)
+            def _():
+                copy_out(j).start()
 
     def advance(turn, carry):
         f, m, s, b = turn, turn - 1, turn - 2, turn - 3
         do_f, do_m = turn < 4, (turn >= 1) & (turn < 5)
         do_s, do_b = (turn >= 2) & (turn < 6), turn >= 3
 
+        @pl.when(do_b)
+        def _():
+            for way in range(2):
+                copy_grad(b, way).wait_recv()
+                copy_on(b, way).start()
+
         @pl.when(do_f)
         def _():
             product(f, 0)
             copy_diag(f, 0).start()
             copy_diag(f, 1).start()
 
+        @pl.when(turn == 1)
+        def _():
+            copy_weight_peer(n, row).start()
+            for j in range(3):
+                copy_weight(j, owners[j]).wait_recv()
+                copy_weight_peer(owners[j], row).start()
+
+        @pl.when(do_s)
+        def _():
+            sum_step(s, 1)
+
         @pl.when(do_m)
         def _():
             gather_step(m, 1)
-
-        @pl.when(do_s)
-        def _():
-            sum_step(s, 1)
-
-        @pl.when(do_b)
-        def _():
-            for way in range(2):
-                copy_grad(b, way).wait_recv()
-                copy_on(b, way).start()
 
         @pl.when(do_f)
         def _():
@@ -335,36 +361,26 @@
             part[f, 2, :half, :] += dx[f]
             copy_part(f, 1).start()
 
+        @pl.when(turn == 0)
+        def _():
+            for j in range(3):
+                copy_weight(j, n).start()
+
+        @pl.when(do_b)
+        def _():
+            for way in range(2):
+                copy_on(b, way).wait_recv()
+            back_product(b, turn == 6, (0, 1))
+
+        @pl.when(do_s)
+        def _():
+            sum_step(s, 2)
+
         @pl.when(do_m)
         def _():
             gather_step(m, 2)
 
-        @pl.when(do_s)
-        def _():
-            sum_step(s, 2)
-
-        @pl.when(turn == 0)
-        def _():
-            copy_weight_peer(n, row).start()
-            for j in range(3):
-                copy_weight(j, owners[j]).wait_recv()
-                copy_weight_peer(owners[j], row).start()
-
-        @pl.when(do_f)
-        def _():
-            for way in range(2):
-                copy_part(f, way).wait_recv()
-            h[f, z] = (part[f, 3] + rx[f] + ry[f]) * scale
-
-            @pl.when(z < 3)
-            def _():
-                copy_hidden(f, z, 0, 0).start()
-
-            @pl.when(z > 0)
-            def _():
-                copy_hidden(f, z, 0, 1).start()
-
-        @pl.when(turn == 0)
+        @pl.when(turn == 1)
         def _():
             for m_ in range(4):
                 copy_weight_peer(m_, peer).wait_recv()
@@ -372,31 +388,9 @@
             w_hi[...], w_lo[...] = halves(whole)
             wt_hi[...], wt_lo[...] = halves(whole.T)
 
-        @pl.when(do_s)
-        def _():
-            ga[s, 3] = gp[z]
-
-            @pl.when(z > 0)
-            def _():
-                copy_sum(s, z, 0, 0).wait_recv()
-                ga[s, 3] += rl[s, z]
-
-            @pl.when(z < 3)
-            def _():
-                copy_sum(s, z, 0, 1).wait_recv()
-                ga[s, 3] += rr[s, z]
-
-            for way in range(2):
-                copy_grad(s, way).start()
-
-        @pl.when(do_m)
-        def _():
-            gather_step(m, 3)
-            dense(m)
-
-        @pl.when(turn == 4)
-        def _():
-            copy_terms().start()
+        @pl.when(do_b)
+        def _():
+            back_product(b, turn == 6, (2, 3))
 
         @pl.when(turn == 5)
         def _():
@@ -405,19 +399,45 @@
             for j in range(3):
                 copy_wsum(j, n).start()
 
-        @pl.when(do_b)
+        @pl.when(do_f)
         def _():
             for way in range(2):
-                copy_on(b, way).wait_recv()
-            grads = ga[b].reshape(CHUNKS * TILE, ga.shape[3])
-            g_hi, g_lo = halves(grads.T * scale)
-            for j in range(4):
-                cols = slice(j * piece, (j + 1) * piece)
-                own_out[:, cols] += dot3(g_hi, g_lo, a_hi[b, :, cols], a_lo[b, :, cols])
-
-                @pl.when(turn == 6)
-                def _():
-                    copy_out(j).start()
+                copy_part(f, way).wait_recv()
+            h[f, z] = (part[f, 3] + rx[f] + ry[f]) * scale
+
+            @pl.when(z < 3)
+            def _():
+                copy_hidden(f, z, 0, 0).start()
+
+            @pl.when(z > 0)
+            def _():
+                copy_hidden(f, z, 0, 1).start()
+
+        @pl.when(do_s)
+        def _():
+            ga[s, 3] = gp[z]
+
+            @pl.when(z > 0)
+            def _():
+                copy_sum(s, z, 0, 0).wait_recv()
+                ga[s, 3] += rl[s, z]
+
+            @pl.when(z < 3)
+            def _():
+                copy_sum(s, z, 0, 1).wait_recv()
+                ga[s, 3] += rr[s, z]
+
+            for way in range(2):
+                copy_grad(s, way).start()
+
+        @pl.when(do_m)
+        def _():
+            gather_step(m, 3)
+            dense(m)
+
+        @pl.when(turn == 4)
+        def _():
+            copy_terms().start()
 
         return carry
 
@@ -473,12 +493,12 @@
     dma = pltpu.SemaphoreType.DMA
     scratch = [
         pltpu.VMEM((c_dev, width), BF16), pltpu.VMEM((c_dev, width), BF16),
-        pltpu.VMEM((CHUNKS, 4 * TILE, c_dev), BF16), pltpu.VMEM((CHUNKS, 4 * TILE, c_dev), BF16),
+        pltpu.VMEM((CHUNKS, 8 * TILE, c_dev), BF16),
         pltpu.VMEM(block, F32),
         pltpu.VMEM((CHUNKS, TILE // 2, width), F32), pltpu.VMEM((CHUNKS, TILE // 2, width), F32),
         pltpu.VMEM((CHUNKS, TILE, width), F32), pltpu.VMEM((CHUNKS, TILE, width), F32),
         pltpu.VMEM(block, F32),
-        pltpu.VMEM((TILE, full), BF16), pltpu.VMEM((TILE, full), BF16),
+        pltpu.VMEM((2 * TILE, full), BF16),
         pltpu.VMEM(block[1:], F32),
         pltpu.VMEM(block, F32), pltpu.VMEM(block, F32), pltpu.VMEM(block, F32),
         pltpu.VMEM((8, full // 8, width), F32),

time: 114 us -> 115 us (level)
    pallas_call x1, Pallas kernels: 107 us -> 108 us  [fused(): pl.pallas_call(functools.partial(fused_kernel, scale), out_shape=[shape(*...]
where the time goes in v3:
time: 115 us
  Pallas kernels  108 us (94%)
  other arithmetic  3.94 us (3%)
  local copies, waits for them, and re-layouts  1.46 us (1%)
  between operations  1.3 us (1%)
    pallas_call x1, Pallas kernels, fused(): pl.pallas_call(functools.partial(fused_kernel, scale), out_shape=[shape(*...  108 us
    add x1, other arithmetic, fused(): return (act, own + other, wg)  3.94 us

profile of v3, /device:TPU:0, one launch (start us, length us, event | category | flops | bytes accessed | tf_op | source)
XLA Modules:
  0.0 115.1 jit_solution(3215644994481708992)
XLA Ops:
  1.3 108.4 %shard_map.76 = (f32[512,256]{1,0:T(8,128)}, f32[256,2048]{1,0:T(8,128)}, f32[256,2048]{1,0:T(8,128)}, f32[128,256]{1,0:T(8,128)}) custom-call(s32[1]{0:T(128)} %bitcast.2.total, s32[2,256]{1,0:T(2,128)} %bitcast.3, f32[256,2048]{1,0:T(8,128)} %x.1, f32[128,256]{1,0:T(8,128)} %w.1, f32[512,256]{1,0:T(8,128)} %cot.1), custom_call_target="tpu_custom_call" | custom-call | flops 12884901888 | bytes 16777216 | tf_op jit(solution)/shard_map/pallas_call | solution.py:516
  109.7 0.0 copy-start
  109.7 0.0 copy-start.1
  109.7 3.9 %add.3 = f32[256,2048]{1,0:T(8,128)} add(f32[256,2048]{1,0:T(8,128)} %get-tuple-element.8, f32[256,2048]{1,0:T(8,128)} %get-tuple-element.9) | non-fusion elementwise | flops 524288 | bytes 6291456 | tf_op jit(solution)/shard_map/add | solution.py:529
  113.7 0.0 copy-done
  113.7 0.8 copy.11
  114.5 0.0 copy-done.1
  114.5 0.7 copy.12
Async XLA Ops:
  109.7 4.0 %copy-start = (f32[512,256]{1,0:T(8,128)S(1)}, f32[512,256]{1,0:T(8,128)}, u32[]{:S(2)}) copy-start(f32[512,256]{1,0:T(8,128)} %get-tuple-element.14) | copy-start | bytes 1572868
  109.7 4.8 %copy-start.1 = (f32[128,256]{1,0:T(8,128)S(1)}, f32[128,256]{1,0:T(8,128)}, u32[]{:S(2)}) copy-start(f32[128,256]{1,0:T(8,128)} %get-tuple-element.16) | copy-start | bytes 393220
